TPU v7x, 256 devices: a whole 4x4x8 slice. The times are simulated.
256 devices in a mesh: blk: 4 (over x_lo, core), wide: 64 (over y, x_hi, z).
Axes of the slice: x: 4 (x_hi: 2, x_lo: 2; x = x_hi * 2 + x_lo), y: 4, z: 8, core: 2. Of those that a mesh axis runs over, the one named last changes fastest.
Arguments:
- src_emb: float32 [4096, 1024], P('blk')
- src_sharp: float32 [4096], P('blk')
- tgt_emb: float32 [262144, 1024], P(('blk', 'wide'))
- tgt_sharp: float32 [262144], P(('blk', 'wide')), may hold values from 4 to 256
- cand_src: int32 [2048, 128], P(('blk', 'wide')), may hold values from 0 to 4095
- cand_tgt: int32 [2048, 128], P(('blk', 'wide')), may hold values from 0 to 127
- cand_count: int32 [2048], P(('blk', 'wide')), may hold values from 1 to 128, as said below
Outputs:
- margins: float32 [2048, 128], P(('blk', 'wide'))
Inputs may be any that keep to these rules, and one draw needn't show every extreme that they name: `cand_count`: some tile uses all 128 slots in every draw.
All inputs are finite; a program needn't handle non-finite values.
Results may differ from a plain program's by a relative error of at most 0.0003.
Values sent between devices are 32-bit elements; how exact they have to be, the bound alone decides.
A program may use at most 128 MiB of HBM per device.

v0:
```python
import jax
import jax.numpy as jnp
from jax import lax
from jax.sharding import PartitionSpec as P

NEIGH = 16


def combined_all(part, axis, combine):
    gathered = jax.tree.map(lambda a: lax.all_gather(a, axis), part)

    def take(source):
        return jax.tree.map(lambda a: lax.dynamic_index_in_dim(a, source, 0, False), gathered)

    return lax.fori_loop(
        1, lax.axis_size(axis), lambda source, state: combine(state, take(source)), take(0)
    )


def normalize(rows):
    return rows / jnp.sqrt(jnp.sum(rows * rows, axis=1, keepdims=True) + 1e-06)


def combine_lse(first, second):
    newmax = jnp.maximum(first[0], second[0])
    return (newmax, first[1] * jnp.exp(first[0] - newmax) + second[1] * jnp.exp(second[0] - newmax))


def per_device(src_emb, src_sharp, tgt_emb, tgt_sharp, cand_src, cand_tgt, cand_count):
    src_unit = normalize(src_emb)
    tgt_unit = normalize(tgt_emb)
    tiles, width = cand_tgt.shape
    total_src = src_emb.shape[0] * lax.axis_size("blk")
    tiled = tgt_unit.reshape(tiles, width, -1)
    paired = jnp.take_along_axis(tiled, cand_tgt[:, :, None], axis=1)
    fmax = jnp.full((total_src,), -1e30, jnp.float32)
    bmax = jnp.full((tgt_emb.shape[0],), -1e30, jnp.float32)
    rows = lax.all_gather(src_unit, "blk", axis=0, tiled=True)
    sharp = lax.all_gather(src_sharp, "blk", axis=0, tiled=True)
    count = rows.shape[0]
    cosine = jnp.dot(tgt_unit, rows.T, precision=lax.Precision.HIGHEST)
    back = tgt_sharp[:, None] * cosine
    top = jnp.maximum(bmax, jnp.max(back, axis=1))
    bsum = jnp.sum(jnp.exp(back - top[:, None]), axis=1)
    ahead = sharp[None, :] * cosine
    peak = jnp.max(ahead, axis=0)
    mass = jnp.sum(jnp.exp(ahead - peak[None, :]), axis=0)
    old_max = fmax
    new_max = jnp.maximum(old_max, peak)
    new_sum = mass * jnp.exp(peak - new_max)
    fmax = new_max
    fsum = new_sum
    sharp_all = sharp
    inside = (cand_src >= 0) & (cand_src < count)
    picked = jnp.take(rows, jnp.clip(cand_src, 0, count - 1), axis=0)
    cand_cos = jnp.where(inside, jnp.sum(picked * paired, axis=-1), 0.0)
    fmax, fsum, sharp_all, bmax, bsum, cand_cos = (fmax, fsum, sharp_all, top, bsum, cand_cos)
    gmax, gsum = combined_all((fmax, fsum), ("blk", "wide"), combine_lse)
    log_neigh = jnp.log(jnp.float32(NEIGH))
    fwd = (gmax + jnp.log(gsum) - log_neigh) / sharp_all
    bwd = (bmax + jnp.log(bsum) - log_neigh) / tgt_sharp
    fwd_cand = jnp.take(fwd, cand_src)
    bwd_cand = jnp.take_along_axis(bwd.reshape(tiles, width), cand_tgt, axis=1)
    denom = jnp.maximum(0.5 * (fwd_cand + bwd_cand), 0.5)
    valid = jnp.arange(width, dtype=jnp.int32)[None, :] < cand_count[:, None]
    return jnp.where(valid, cand_cos / denom, 0.0)


def solution(mesh):
    placed = (
        P("blk", None),
        P("blk"),
        P(("blk", "wide"), None),
        P(("blk", "wide")),
        P(("blk", "wide"), None),
        P(("blk", "wide"), None),
        P(("blk", "wide")),
    )
    return jax.shard_map(
        per_device, mesh=mesh, in_specs=placed, out_specs=P(("blk", "wide"), None), check_vma=False
    )
```

profile of v0, /device:TPU:1, one launch (start us, length us, event | category | flops | bytes accessed | tf_op | source)
XLA Modules:
  0.0 1941.0 jit_solution(640253729421964220)
XLA Ops:
  6.5 2.7 multiply_reduce_fusion.4
  10.0 2.4 broadcast_divide_fusion.1
  13.1 8.3 all_gather.15
  21.4 2.5 multiply_reduce_fusion.3
  24.0 2.4 broadcast_divide_fusion
  26.4 144.1 %all-gather.6.cloned.1.call-done = f32[4096,1024]{1,0:T(8,128)} async-done(((f32[1024,1024]{1,0:T(8,128)}), f32[4096,1024]{1,0:T(8,128)}) %all-gather.6.cloned.1.call-update) | async-done | bytes 16777232 | tf_op jit(solution)/shard_map/all_gather | solution.py:38
  170.4 58.9 %multiply_reduce_fusion.1 = (f32[4096]{0:T(1024)S(1)}, f32[1024]{0:T(1024)S(1)}, f32[1024,4096]{1,0:T(8,128)S(1)}) fusion(f32[4096]{0:T(1024)S(1)} %all_gather.15, f32[1024]{0:T(1024)S(1)} %copy-done.3, f32[1024,1024]{1,0:T(8,128)} %broadcast_divide_fusion, f32[4096,1024]{1,0:T(8,128)} %all-gather.6.cloned.1.call-done), kind=kOutput, calls=%fused_computation.10 | convolution fusion | flops 51556380672 | bytes 37789696 | tf_op jit(solution)/shard_map/dot_general | solution.py:41
  229.3 6.4 exponential_reduce_fusion.1
  237.2 20.7 %gather_fusion.2 = f32[1024,1024]{1,0:T(8,128)} fusion(f32[8,128,1024]{2,1,0:T(8,128)} %bitcast.53, s32[1024]{0:T(1024)S(1)} %fusion.8), kind=kCustom, calls=%fused_computation.2 | custom fusion | bytes 8396800 | tf_op jit(solution)/shard_map/jit(take_along_axis)/gather | solution.py:35
  257.9 4.5 gather_fusion.3
  262.5 12.2 gather_fusion
  274.7 3.9 multiply_reduce_fusion.2
  278.6 665.7 %all-gather.8.cloned.1.call-done = f32[256,1,4096]{2,1,0:T(1,128)} async-done(((f32[1,1,4096]{2,1,0:T(1,128)}), f32[256,1,4096]{2,1,0:T(1,128)}) %all-gather.8.cloned.1.call-update) | async-done | bytes 4194320 | tf_op jit(solution)/shard_map/all_gather | solution.py:10
  944.3 7.9 copy.13
  952.2 700.5 %all-gather.10.cloned.1.call-done = f32[256,1,4096]{2,1,0:T(1,128)} async-done(((f32[1,1,4096]{2,1,0:T(1,128)}), f32[256,1,4096]{2,1,0:T(1,128)}) %all-gather.10.cloned.1.call-update) | async-done | bytes 4194320 | tf_op jit(solution)/shard_map/all_gather | solution.py:10
  1652.7 8.0 copy.12
  1660.8 266.8 %while.17 = (s32[]{:T(128)}, f32[4096]{0:T(1024)S(1)}, f32[4096]{0:T(1024)S(1)}, f32[256,4096]{1,0:T(8,128)}, f32[256,4096]{1,0:T(8,128)}, /*index=5*/s32[]{:T(128)}, s32[]{:T(128)}, s32[]{:T(128)}) while((s32[]{:T(128)}, f32[4096]{0:T(1024)S(1)}, f32[4096]{0:T(1024)S(1)}, f32[256,4096]{1,0:T(8,128)}, f32[256,4096]{1,0:T(8,128)}, ...), condition=%wide.region_6.7_spmd, body=%wide.region_5.6_spmd.sunk | while | flops 24581 | bytes 163971 | solution.py:15
  1661.8 1.0 constant_dynamic-slice_fusion.3
  1662.9 1.0 constant_dynamic-slice_fusion.3
  1663.9 1.0 constant_dynamic-slice_fusion.3
  1665.0 1.0 constant_dynamic-slice_fusion.3
  1667.1 1.0 constant_dynamic-slice_fusion.3
  1668.1 1.0 constant_dynamic-slice_fusion.3
  1669.1 1.0 constant_dynamic-slice_fusion.3
  1670.2 1.0 constant_dynamic-slice_fusion.3
  1672.3 1.0 constant_dynamic-slice_fusion.3
  1673.3 1.0 constant_dynamic-slice_fusion.3
  1674.4 1.0 constant_dynamic-slice_fusion.3
  1677.5 1.0 constant_dynamic-slice_fusion.3
  1678.6 1.0 constant_dynamic-slice_fusion.3
  1679.6 1.0 constant_dynamic-slice_fusion.3
  1927.6 6.2 gather_fusion.1
  (530 shorter events, 249.8 us)
Async XLA Ops:
  6.5 163.9 %all-gather.6.cloned.1.call-start = ((), (), s32[]{:S(2)}) async-start(), calls=%async_computation | async-start | bytes 20971520 | tf_op jit(solution)/shard_map/all_gather | solution.py:38
  6.5 3.4 copy-start
  12.4 0.7 copy-start.5
  12.4 931.9 %all-gather.8.cloned.1.call-start = ((), (), s32[]{:S(2)}) async-start(), calls=%async_computation.1 | async-start | bytes 4210688 | tf_op jit(solution)/shard_map/all_gather | solution.py:10
  13.1 10.9 copy-start.1
  23.9 146.5 %copy-start.3 = (f32[1024]{0:T(1024)S(1)}, f32[1024]{0:T(1024)}, u32[]{:S(2)}) copy-start(f32[1024]{0:T(1024)} %param.12) | copy-start | bytes 12292
  229.3 7.8 copy-start.4
  236.4 1416.3 %all-gather.10.cloned.1.call-start = ((), (), s32[]{:S(2)}) async-start(), calls=%async_computation.2 | async-start | bytes 4210688 | tf_op jit(solution)/shard_map/all_gather | solution.py:10
  237.1 20.8 %copy-start.2 = (s32[8,128]{1,0:T(8,128)S(1)}, s32[8,128]{1,0:T(8,128)}, u32[]{:S(2)}) copy-start(s32[8,128]{1,0:T(8,128)} %param.13) | copy-start | bytes 12292
  952.2 708.5 %slice-start = ((f32[256,1,4096]{2,1,0:T(1,128)}), f32[1,1,4096]{2,1,0:T(1,128)S(1)}, s32[]{:S(2)}) async-start(f32[256,1,4096]{2,1,0:T(1,128)} %all-gather.8.cloned.1.call-done), calls=%async_computation.3 | async-start | bytes 32768 | tf_op jit(solution)/shard_map/jit(dynamic_index_in_dim)/dynamic_slice | solution.py:13
  1652.7 8.0 slice-start.1
  1660.8 273.0 %copy-start.6 = (s32[8]{0:T(128)S(1)}, s32[8]{0:T(128)}, u32[]{:S(2)}) copy-start(s32[8]{0:T(128)} %param.15) | copy-start | bytes 100
Sparse Core Ops, SparseCore 0:
  12.5 157.8 all-gather.5
  236.5 707.7 all-gather.7
  946.2 706.4 all-gather.9
where the time goes:
time: 1950 us; the launch traced here: 1940 us
  waiting for transfers between devices  1510 us (77%)
  local copies, waits for them, and re-layouts  315 us (16%)
  matrix products  58.9 us (3%)
  other arithmetic  27.4 us (1%)
    all_gather x2, waiting for transfers between devices, combined_all(): gathered = jax.tree.map(lambda a: lax.all_gather(a, axis), part)  1370 us
    dynamic_slice x259, local copies, waits for them, and re-layouts, take(): lax.dynamic_index_in_dim(a, source, 0, False)  254 us
    all_gather x1, waiting for transfers between devices, per_device(): rows = lax.all_gather(src_unit, 'blk', axis=0, tiled=True)  144 us
    dot_general x1, matrix products, per_device(): cosine = jnp.dot(tgt_unit, rows.T, precision=lax.Precision.HIGHEST)  58.9 us
  transfers between devices with their start and end apart: 3, of which 3 were waited for; matrix products, arithmetic and copies ran while one was open for 3% of the time, Pallas kernels for 0%

commit v1 on v0

v1 whole, which is shorter than its diff:
```python
import jax
import jax.numpy as jnp
from jax import lax
from jax.experimental import pallas as pl
from jax.experimental.pallas import tpu as pltpu
from jax.sharding import PartitionSpec as P

LOG2E = 1.4426950408889634
LN2 = 0.6931471805599453
MESH = pl.DeviceIdType.MESH
D = 1024
ROWS = 1024
UNIT = 128
HALF = 512
SUB = 64
ROUNDS = 4
NTILE = 256
RELAY_STEP = (6, 12, 17, 23)
MATE_STEP = (12, 17, 23, 28)


def log2(v):
    return jnp.log(v) * LOG2E


def combine(parts):
    top = jnp.max(parts, axis=0)
    return top + log2(jnp.sum(jnp.exp2(parts - top[None]), axis=0))


def kernel(
    src_hbm, sharp_in, tgt_hbm, tsharp_ref, cand_smem, cand_ref, ctgt_ref, count_ref, out_ref,
    srcall, cos, tgt_raw, t_hi, t_lo, s_hi, s_lo, sharp_all, lse, part_a, part_b, fwd_all,
    top_y, sum_y, bwd8, picked, pair8,
    load_sem, own_send, own_recv, x_send, x_recv, y_send, y_recv, mx_send, mx_recv, my_send, my_recv,
    sh_send, sh_recv, a_send, a_recv, b_send, b_recv, c_send, c_recv,
):
    b = lax.axis_index("blk")
    w = lax.axis_index("wide")
    x_lo, core = b // 2, b % 2
    y, x_hi, z = w // 16, (w // 8) % 2, w % 8
    x = x_hi * 2 + x_lo
    par = y % 2
    opp = 1 - x_lo
    mate_b = x_lo * 2 + 1 - core
    opp_b = opp * 2 + core
    opp_mate_b = opp * 2 + 1 - core

    def at(xx, yy):
        return ((xx % 2) * 2 + core, yy * 16 + (xx // 2) * 8 + z)

    right, left = at((x + 1) % 4, y), at((x + 3) % 4, y)
    up, down = at(x, (y + 1) % 4), at(x, (y + 3) % 4)
    mate = (mate_b, w)
    me_a = core * 8 + z
    me_b = x_lo * 8 + w // 8

    def peer_a(d):
        a = (me_a + d) % 16
        return (x_lo * 2 + a // 8, (w // 8) * 8 + a % 8)

    def peer_b(d):
        g = (me_b + d) % 16
        return ((g // 8) * 2 + core, (g % 8) * 8 + z)

    own_base = b * ROWS
    first = par * HALF
    second = (1 - par) * HALF

    def load_src(i, offset):
        return pltpu.make_async_copy(
            src_hbm.at[pl.ds(offset, HALF)],
            srcall.at[pl.ds(pl.multiple_of(own_base + offset, HALF), HALF)],
            load_sem.at[i],
        )

    loads = [load_src(0, first), load_src(1, second)]
    load_tgt = pltpu.make_async_copy(tgt_hbm, tgt_raw, load_sem.at[2])
    for load in loads:
        load.start()
    load_tgt.start()

    barrier = pltpu.get_barrier_semaphore()

    def greet(d, _):
        pl.semaphore_signal(barrier, inc=1, device_id=peer_a(d), device_id_type=MESH)
        pl.semaphore_signal(barrier, inc=1, device_id=peer_b(d), device_id_type=MESH)
        return 0

    lax.fori_loop(1, 16, greet, 0)
    pl.semaphore_signal(barrier, inc=1, device_id=(opp_mate_b, w), device_id_type=MESH)

    def unit_rows(ref, start):
        def body(i, _):
            at_rows = pl.ds(pl.multiple_of(start + i * 32, 32), 32)
            rows = ref[at_rows, :]
            norm = jnp.sum(rows * rows, axis=1, keepdims=True) + 1e-06
            ref[at_rows, :] = rows / jnp.sqrt(norm)
            return 0

        lax.fori_loop(0, HALF // 32, body, 0)

    loads[0].wait()
    unit_rows(srcall, own_base + first)
    pl.semaphore_wait(barrier, 31)

    def remote(rows, count, send, recv, where):
        there = srcall.at[pl.ds(pl.multiple_of(rows, SUB), count)]
        return pltpu.make_async_remote_copy(
            src_ref=there, dst_ref=there, send_sem=send, recv_sem=recv,
            device_id=where, device_id_type=MESH,
        )

    def x_copies(k):
        at_row = own_base + first + k * UNIT
        return (
            remote(at_row, SUB, x_send.at[k, 0], x_recv.at[k, 0], right),
            remote(at_row + SUB, SUB, x_send.at[k, 1], x_recv.at[k, 1], left),
        )

    def x_arrivals(k):
        at_row = opp_b * ROWS + first + k * UNIT
        return (
            remote(at_row, SUB, x_send.at[k, 0], x_recv.at[k, 0], right),
            remote(at_row + SUB, SUB, x_send.at[k, 1], x_recv.at[k, 1], left),
        )

    def y_copies(k):
        at_row = opp_b * ROWS + first + k * UNIT
        return (
            remote(at_row, SUB, y_send.at[k, 0], y_recv.at[k, 0], up),
            remote(at_row + SUB, SUB, y_send.at[k, 1], y_recv.at[k, 1], down),
        )

    def y_arrivals(k):
        at_row = opp_b * ROWS + second + k * UNIT
        return (
            remote(at_row, SUB, y_send.at[k, 0], y_recv.at[k, 0], up),
            remote(at_row + SUB, SUB, y_send.at[k, 1], y_recv.at[k, 1], down),
        )

    def mx_copy(k, block):
        return remote(block * ROWS + first + k * UNIT, UNIT, mx_send.at[k], mx_recv.at[k], mate)

    def my_copy(k, block):
        return remote(block * ROWS + second + k * UNIT, UNIT, my_send.at[k], my_recv.at[k], mate)

    def own_copy(i, block):
        return remote(block * ROWS + (first, second)[i], HALF, own_send.at[i], own_recv.at[i], mate)

    def sharp_copy(i, block, where):
        there = sharp_all.at[pl.ds(block * 8, 8)]
        return pltpu.make_async_remote_copy(
            src_ref=there, dst_ref=there, send_sem=sh_send.at[i], recv_sem=sh_recv.at[i],
            device_id=where, device_id_type=MESH,
        )

    for k in range(ROUNDS):
        for copy in x_copies(k):
            copy.start()
    sharp_all[pl.ds(b * 8, 8)] = sharp_in[...]
    sharp_to = ((mate_b, w), (opp_b, w), (opp_mate_b, w))
    for i, where in enumerate(sharp_to):
        sharp_copy(i, b, where).start()
    own_copy(0, b).start()
    loads[1].wait()
    unit_rows(srcall, own_base + second)
    own_copy(1, b).start()

    load_tgt.wait()

    def split_target(t):
        rows = tgt_raw[t * 128:(t + 1) * 128, :]
        norm = jnp.sum(rows * rows, axis=1, keepdims=True) + 1e-06
        turned = (rows / jnp.sqrt(norm)).T
        high = turned.astype(jnp.bfloat16)
        t_hi[:, t * 128:(t + 1) * 128] = high
        t_lo[:, t * 128:(t + 1) * 128] = (turned - high.astype(jnp.float32)).astype(jnp.bfloat16)

    for t in range(8):
        split_target(t)
    top_y[...] = jnp.full(top_y.shape, -1e30, jnp.float32)
    sum_y[...] = jnp.zeros(sum_y.shape, jnp.float32)
    for i, block in enumerate((mate_b, opp_b, opp_mate_b)):
        sharp_copy(i, block, sharp_to[i]).wait_recv()

    eye = lax.broadcasted_iota(jnp.int32, (128, 128), 0) == lax.broadcasted_iota(jnp.int32, (128, 128), 1)

    def unit_of(j, i):
        block = jnp.where(j < 2, b, mate_b)
        near = block * 8 + (j % 2) * 4 + i
        far_block = opp_b if i < 2 else opp_mate_b
        far = far_block * 8 + (par if i % 2 == 0 else 1 - par) * 4 + (j - 4)
        return jnp.where(j < 4, near, far)

    def step(s, _):
        j = s // 4
        n = s % 4
        for k in range(ROUNDS):
            @pl.when(s == RELAY_STEP[k])
            def _(k=k):
                for copy in x_arrivals(k):
                    copy.wait_recv()
                for copy in y_copies(k):
                    copy.start()
                mx_copy(k, opp_b).start()

            @pl.when(s == MATE_STEP[k])
            def _(k=k):
                for copy in y_arrivals(k):
                    copy.wait_recv()
                my_copy(k, opp_b).start()

            @pl.when(s == 16 + 4 * k)
            def _(k=k):
                mx_copy(k, opp_mate_b).wait_recv()
                my_copy(k, opp_mate_b).wait_recv()

        @pl.when(s == 8)
        def _():
            for i in range(2):
                own_copy(i, mate_b).wait_recv()

        @pl.when(n == 0)
        def _():
            for i in range(4):
                rows = srcall[pl.ds(pl.multiple_of(unit_of(j, i) * UNIT, UNIT), UNIT), :]
                high = rows.astype(jnp.bfloat16)
                s_hi[i * UNIT:(i + 1) * UNIT, :] = high
                s_lo[i * UNIT:(i + 1) * UNIT, :] = (rows - high.astype(jnp.float32)).astype(jnp.bfloat16)

        at_n = pl.ds(pl.multiple_of(n * NTILE, NTILE), NTILE)
        high_t, low_t = t_hi[:, at_n], t_lo[:, at_n]
        tile = jnp.dot(s_hi[...], high_t, preferred_element_type=jnp.float32)
        tile += jnp.dot(s_hi[...], low_t, preferred_element_type=jnp.float32)
        tile += jnp.dot(s_lo[...], high_t, preferred_element_type=jnp.float32)
        for i in range(4):
            at_unit = pl.ds(pl.multiple_of(unit_of(j, i) * UNIT, UNIT), UNIT)
            for part in range(NTILE // 128):
                cos[n * (NTILE // 128) + part, at_unit, :] = tile[i * UNIT:(i + 1) * UNIT, part * 128:(part + 1) * 128]
        scale = tsharp_ref[:, at_n] * LOG2E
        old = top_y[:, at_n]
        new = jnp.maximum(old, scale * jnp.max(tile, axis=0, keepdims=True))
        mass = jnp.sum(jnp.exp2(tile * scale - new), axis=0, keepdims=True)
        sum_y[:, at_n] = sum_y[:, at_n] * jnp.exp2(old - new) + mass
        top_y[:, at_n] = new

        @pl.when(n == 3)
        def _():
            for i in range(4):
                unit = unit_of(j, i)
                ahead = cos[:, pl.ds(pl.multiple_of(unit * UNIT, UNIT), UNIT), :]
                row = jnp.broadcast_to(sharp_all[unit] * LOG2E, (128, 128))
                column = jnp.sum(jnp.where(eye, row, 0.0), axis=1, keepdims=True)
                ahead = ahead * column[None]
                peak = jnp.max(jnp.max(ahead, axis=0), axis=1, keepdims=True)
                total = peak + log2(jnp.sum(jnp.sum(jnp.exp2(ahead - peak[None]), axis=0), axis=1, keepdims=True))
                lse[unit] = jnp.sum(jnp.where(eye, jnp.broadcast_to(total, (128, 128)), 0.0), axis=0, keepdims=True)

        return 0

    lax.fori_loop(0, 32, step, 0)

    def to_a(d):
        owner = (me_a + d) % 16
        return pltpu.make_async_remote_copy(
            src_ref=lse.at[pl.ds(owner * 2, 2)], dst_ref=part_a.at[d - 1], send_sem=a_send, recv_sem=a_recv,
            device_id=peer_a(d), device_id_type=MESH,
        )

    def start_a(d, _):
        to_a(d).start()
        return 0

    lax.fori_loop(1, 16, start_a, 0)

    def pick(t):
        def body(i, _):
            for u in range(16):
                slot = i * 16 + u
                picked[pl.ds(slot, 1), :] = cos[t, pl.ds(cand_smem[t, slot], 1), :]
            return 0

        lax.fori_loop(0, 8, body, 0)
        want = lax.broadcasted_iota(jnp.int32, (128, 128), 0) == ctgt_ref[t:t + 1, :]
        pair8[t:t + 1, :] = jnp.sum(jnp.where(want, picked[...].T, 0.0), axis=0, keepdims=True)

    for t in range(4):
        pick(t)
    pltpu.make_async_copy(part_a, part_a, a_recv).wait()
    mine = lse[pl.ds(me_a * 2, 2)]
    part_b[0] = combine(jnp.concatenate([part_a[...], mine[None]], axis=0))

    def start_b(d, _):
        pltpu.make_async_remote_copy(
            src_ref=part_b.at[0], dst_ref=part_b.at[d], send_sem=b_send, recv_sem=b_recv,
            device_id=peer_b(d), device_id_type=MESH,
        ).start()
        return 0

    lax.fori_loop(1, 16, start_b, 0)
    for t in range(4, 8):
        pick(t)
    scale_y = tsharp_ref[...]
    bwd = (top_y[...] + log2(sum_y[...]) - 4.0) * LN2 / scale_y
    for t in range(8):
        bwd8[t:t + 1, :] = bwd[:, t * 128:(t + 1) * 128]
    pltpu.make_async_copy(part_b.at[pl.ds(1, 15)], part_b.at[pl.ds(1, 15)], b_recv).wait()
    fwd_all[me_a] = (combine(part_b[...]) - 4.0) * LN2 / sharp_all[pl.ds(me_a * 2, 2)]

    def start_c(d, _):
        there = fwd_all.at[me_a]
        pltpu.make_async_remote_copy(
            src_ref=there, dst_ref=there, send_sem=c_send, recv_sem=c_recv,
            device_id=peer_a(d), device_id_type=MESH,
        ).start()
        return 0

    lax.fori_loop(1, 16, start_c, 0)

    for k in range(ROUNDS):
        for copy in (*x_copies(k), *y_copies(k)):
            copy.wait_send()
        mx_copy(k, opp_b).wait_send()
        my_copy(k, opp_b).wait_send()
    for i in range(2):
        own_copy(i, b).wait_send()
    for i, where in enumerate(sharp_to):
        sharp_copy(i, b, where).wait_send()
    pltpu.make_async_copy(part_a, part_a, a_send).wait()
    pltpu.make_async_copy(part_b.at[pl.ds(1, 15)], part_b.at[pl.ds(1, 15)], b_send).wait()

    def lookup(table, index):
        return jnp.take_along_axis(table, index, axis=1, mode="promise_in_bounds")

    bwd_cand = lookup(bwd8[...], ctgt_ref[...])
    sources = cand_ref[...]
    low, high = sources % 128, sources // 128
    counts = jnp.zeros((8, 128), jnp.int32)
    tile_id = lax.broadcasted_iota(jnp.int32, (8, 128), 0)
    for t in range(8):
        counts = jnp.where(tile_id == t, count_ref[t], counts)
    valid = lax.broadcasted_iota(jnp.int32, (8, 128), 1) < counts

    pltpu.make_async_copy(part_a, part_a, c_recv).wait()
    pltpu.make_async_copy(part_a, part_a, c_send).wait()
    fwd_cand = jnp.zeros((8, 128), jnp.float32)
    for r in range(32):
        row = jnp.broadcast_to(fwd_all[r // 2, r % 2], (8, 128))
        fwd_cand = jnp.where(high == r, lookup(row, low), fwd_cand)
    denom = jnp.maximum(0.5 * (fwd_cand + bwd_cand), 0.5)
    out_ref[...] = jnp.where(valid, pair8[...] / denom, 0.0)


def per_device(src_emb, src_sharp, tgt_emb, tgt_sharp, cand_src, cand_tgt, cand_count):
    vmem = pl.BlockSpec(memory_space=pltpu.VMEM)
    smem = pl.BlockSpec(memory_space=pltpu.SMEM)
    hbm = pl.BlockSpec(memory_space=pl.ANY)
    dma = pltpu.SemaphoreType.DMA
    f32, bf16 = jnp.float32, jnp.bfloat16
    return pl.pallas_call(
        kernel,
        out_shape=jax.ShapeDtypeStruct((8, 128), f32),
        in_specs=[hbm, vmem, hbm, vmem, smem, vmem, vmem, smem],
        out_specs=vmem,
        scratch_shapes=[
            pltpu.VMEM((4 * ROWS, D), f32),
            pltpu.VMEM((8, 4 * ROWS, 128), f32),
            pltpu.VMEM((ROWS, D), f32),
            pltpu.VMEM((D, ROWS), bf16),
            pltpu.VMEM((D, ROWS), bf16),
            pltpu.VMEM((HALF, D), bf16),
            pltpu.VMEM((HALF, D), bf16),
            pltpu.VMEM((32, 1, 128), f32),
            pltpu.VMEM((32, 1, 128), f32),
            pltpu.VMEM((15, 2, 1, 128), f32),
            pltpu.VMEM((16, 2, 1, 128), f32),
            pltpu.VMEM((16, 2, 1, 128), f32),
            pltpu.VMEM((1, ROWS), f32),
            pltpu.VMEM((1, ROWS), f32),
            pltpu.VMEM((8, 128), f32),
            pltpu.VMEM((128, 128), f32),
            pltpu.VMEM((8, 128), f32),
            dma((3,)), dma((2,)), dma((2,)), dma((4, 2)), dma((4, 2)), dma((4, 2)), dma((4, 2)),
            dma((4,)), dma((4,)), dma((4,)), dma((4,)), dma((3,)), dma((3,)),
            dma, dma, dma, dma, dma, dma,
        ],
        compiler_params=pltpu.CompilerParams(
            collective_id=0, has_side_effects=True, vmem_limit_bytes=60 * 1024 * 1024
        ),
        cost_estimate=pl.CostEstimate(flops=6 * 4096 * 1024 * 1024, bytes_accessed=8 << 20, transcendentals=8 << 20),
    )(
        src_emb, src_sharp.reshape(8, 1, 128), tgt_emb, tgt_sharp.reshape(1, ROWS),
        cand_src, cand_src, cand_tgt, cand_count,
    )


def solution(mesh):
    placed = (
        P("blk", None),
        P("blk"),
        P(("blk", "wide"), None),
        P(("blk", "wide")),
        P(("blk", "wide"), None),
        P(("blk", "wide"), None),
        P(("blk", "wide")),
    )
    return jax.shard_map(
        per_device, mesh=mesh, in_specs=placed, out_specs=P(("blk", "wide"), None), check_vma=False
    )
```

time: 1950 us -> 104 us (0.05)
  waiting for transfers between devices: 1510 us -> 0 us
  local copies, waits for them, and re-layouts: 315 us -> 1.28 us
  Pallas kernels: 0 us -> 102 us
  matrix products: 58.9 us -> 0 us
  other arithmetic: 27.4 us -> 0 us
    all_gather x3 -> x0, waiting for transfers between devices: 1510 us -> none  [the longest x2 1370 us: combined_all(): gathered = jax.tree.map(lambda a: lax.all_gather(a, axis), part)]
    dynamic_slice x259 -> x0, local copies, waits for them, and re-layouts: 254 us -> none  [take(): lax.dynamic_index_in_dim(a, source, 0, False)]
    pallas_call x0 -> x1, Pallas kernels: none -> 102 us  [per_device(): pl.pallas_call(kernel, out_shape=jax.ShapeDtypeStruct((8, 128), f32), in_...]
    dot_general x1 -> x0, matrix products: 58.9 us -> none  [per_device(): cosine = jnp.dot(tgt_unit, rows.T, precision=lax.Precision.HIGHEST)]
    gather x4 -> x0, local copies, waits for them, and re-layouts: 43.6 us -> none  [the longest x1 20.7 us: per_device(): paired = jnp.take_along_axis(tiled, cand_tgt[:, :, None], axis=1)]
  transfers between devices with their start and end apart: 3 -> 0, of which waited for: 3 -> 0; matrix products, arithmetic and copies ran while one was open for 3% -> 0% of each run, Pallas kernels for 0% -> 0%
where the time goes in v1:
time: 104 us; the launch traced here: 103 us
  Pallas kernels  102 us (98%)
  local copies, waits for them, and re-layouts  1.28 us (1%)
    pallas_call x1, Pallas kernels, per_device(): pl.pallas_call(kernel, out_shape=jax.ShapeDtypeStruct((8, 128), f32), in_...  102 us

profile of v1, /device:TPU:1, one launch (start us, length us, event | category | flops | bytes accessed | tf_op | source)
XLA Modules:
  0.0 103.4 jit_solution(9858902497255251972)
XLA Ops:
  0.0 102.2 %shard_map.73 = f32[8,128]{1,0:T(8,128)} custom-call(f32[1024,1024]{1,0:T(8,128)} %src_hbm.1, f32[8,1,128]{2,1,0:T(1,128)} %bitcast.2, f32[1024,1024]{1,0:T(8,128)} %tgt_hbm.1, f32[1,1024]{1,0:T(1,128)} %bitcast.3, s32[8,128]{1,0:T(8,128)} %cand_ref.1, s32[8,128]{1,0:T(8,128)} %cand_ref.1, s32[8,128]{1,0:T(8,128)} %ctgt_ref.1, s32[8]{0:T(128)} %count_ref.1), custom_call_target="tpu_custom_call" | custom-call | flops 25769803776 | bytes 8388608 | tf_op jit(solution)/shard_map/pallas_call | solution.py:361
  102.2 1.3 %copy.9 = f32[8,128]{1,0:T(8,128)} copy(f32[8,128]{1,0:T(8,128)} %shard_map.73) | data formatting | bytes 8192

commit v2 on v1

v2 whole, which is shorter than its diff:
```python
import jax
import jax.numpy as jnp
from jax import lax
from jax.experimental import pallas as pl
from jax.experimental.pallas import tpu as pltpu
from jax.sharding import PartitionSpec as P

LOG2E = 1.4426950408889634
LN2 = 0.6931471805599453
MESH = pl.DeviceIdType.MESH
D = 1024
ROWS = 1024
UNIT = 128
HALF = 512
QUARTER = 256
PIECE = 32
X_SLOT = (-1, 2, 4, 5)
RELAY_SLOT = (5, 7, 9, 10)
CROSS_SLOT = (12, 15)
MATE_SLOT = (17, 20)
ROUND_SLOT = (12, 15, 18, 21)


def log2(v):
    return jnp.log(v) * LOG2E


def combine(parts):
    top = jnp.max(parts, axis=0)
    return top + log2(jnp.sum(jnp.exp2(parts - top[None]), axis=0))


def kernel(
    src_hbm, sharp_in, tgt_hbm, tsharp_ref, cand_smem, cand_ref, ctgt_ref, count_ref, out_ref,
    srcall, cos, tgt_raw, t_hi, t_lo, s_hi, s_lo, sharp_all, lse, part_a, part_b, fwd_all,
    buf_a, buf_b, scale_x, peak_x, top_y, sum_y, bwd8, picked, pair8,
    load_sem, own_send, own_recv, x_send, x_recv, y_send, y_recv, z_send, z_recv,
    dy_send, dy_recv, dz_send, dz_recv, m_send, m_recv,
    sh_send, sh_recv, a_send, a_recv, b_send, b_recv, c_send, c_recv,
):
    b = lax.axis_index("blk")
    w = lax.axis_index("wide")
    x_lo, core = b // 2, b % 2
    y, x_hi, z = w // 16, (w // 8) % 2, w % 8
    x = x_hi * 2 + x_lo
    row_q, col_q = y % 2, z % 2
    q_x = row_q * 2 + col_q
    q_y = (1 - row_q) * 2 + col_q
    q_z = row_q * 2 + 1 - col_q
    q_d = (1 - row_q) * 2 + 1 - col_q
    opp = 1 - x_lo
    mate_b = x_lo * 2 + 1 - core
    opp_b = opp * 2 + core
    opp_mate_b = opp * 2 + 1 - core

    def at(xx, yy, zz):
        return ((xx % 2) * 2 + core, yy * 16 + (xx // 2) * 8 + zz)

    x_next, x_prev = at((x + 1) % 4, y, z), at((x + 3) % 4, y, z)
    y_next, y_prev = at(x, (y + 1) % 4, z), at(x, (y + 3) % 4, z)
    z_next, z_prev = at(x, y, (z + 1) % 8), at(x, y, (z + 7) % 8)
    mate = (mate_b, w)
    me_a = core * 8 + z
    me_b = x_lo * 8 + w // 8

    def peer_a(d):
        a = (me_a + d) % 16
        return (x_lo * 2 + a // 8, (w // 8) * 8 + a % 8)

    def peer_b(d):
        g = (me_b + d) % 16
        return ((g // 8) * 2 + core, (g % 8) * 8 + z)

    own_base = b * ROWS

    def load_src(i):
        return pltpu.make_async_copy(
            src_hbm.at[pl.ds(i * HALF, HALF)],
            srcall.at[pl.ds(pl.multiple_of(own_base + i * HALF, HALF), HALF)],
            load_sem.at[i],
        )

    loads = [load_src(0), load_src(1)]
    load_tgt = pltpu.make_async_copy(tgt_hbm, tgt_raw, load_sem.at[2])
    for load in loads:
        load.start()
    load_tgt.start()

    barrier = pltpu.get_barrier_semaphore()

    def greet(d, _):
        pl.semaphore_signal(barrier, inc=1, device_id=peer_a(d), device_id_type=MESH)
        pl.semaphore_signal(barrier, inc=1, device_id=peer_b(d), device_id_type=MESH)
        return 0

    lax.fori_loop(1, 16, greet, 0)
    pl.semaphore_signal(barrier, inc=1, device_id=(opp_mate_b, w), device_id_type=MESH)

    def unit_rows(ref, start):
        def body(i, _):
            at_rows = pl.ds(pl.multiple_of(start + i * 32, 32), 32)
            rows = ref[at_rows, :]
            norm = jnp.sum(rows * rows, axis=1, keepdims=True) + 1e-06
            ref[at_rows, :] = rows / jnp.sqrt(norm)
            return 0

        lax.fori_loop(0, HALF // 32, body, 0)

    def remote(rows, count, send, recv, where):
        there = srcall.at[pl.ds(pl.multiple_of(rows, PIECE), count)]
        return pltpu.make_async_remote_copy(
            src_ref=there, dst_ref=there, send_sem=send, recv_sem=recv,
            device_id=where, device_id_type=MESH,
        )

    def piece(block, quarter, k, side):
        return block * ROWS + quarter * QUARTER + (k // 2) * UNIT + side * 64 + (k % 2) * PIECE

    def both(block, quarter, k, send, recv, where):
        return tuple(
            remote(piece(block, quarter, k, side), PIECE, send.at[k, side], recv.at[k, side], where[side])
            for side in range(2)
        )

    along_x, along_y, along_z = (x_next, x_prev), (y_next, y_prev), (z_next, z_prev)

    def x_copies(k, block):
        return both(block, q_x, k, x_send, x_recv, along_x)

    def y_copies(k, quarter):
        return both(opp_b, quarter, k, y_send, y_recv, along_y)

    def z_copies(k, quarter):
        return both(opp_b, quarter, k, z_send, z_recv, along_z)

    def cross_copies(u, over_y, over_z):
        return (
            *(remote(piece(opp_b, over_y, 2 * u, side), PIECE, dy_send.at[u, side], dy_recv.at[u, side], along_y[side]) for side in range(2)),
            *(remote(piece(opp_b, over_z, 2 * u + 1, side), PIECE, dz_send.at[u, side], dz_recv.at[u, side], along_z[side]) for side in range(2)),
        )

    quarters = (q_x, q_y, q_z, q_d)

    def mate_copy(i, u, block):
        return remote(block * ROWS + quarters[i] * QUARTER + u * UNIT, UNIT, m_send.at[i, u], m_recv.at[i, u], mate)

    def own_copy(i, block):
        return remote(block * ROWS + i * HALF, HALF, own_send.at[i], own_recv.at[i], mate)

    def sharp_copy(i, block, where):
        there = sharp_all.at[pl.ds(block * 8, 8)]
        return pltpu.make_async_remote_copy(
            src_ref=there, dst_ref=there, send_sem=sh_send.at[i], recv_sem=sh_recv.at[i],
            device_id=where, device_id_type=MESH,
        )

    for i in range(2):
        loads[i].wait()
        unit_rows(srcall, own_base + i * HALF)

    load_tgt.wait()

    def split_target(t):
        rows = tgt_raw[t * 128:(t + 1) * 128, :]
        norm = jnp.sum(rows * rows, axis=1, keepdims=True) + 1e-06
        turned = (rows / jnp.sqrt(norm)).T
        high = turned.astype(jnp.bfloat16)
        t_hi[:, t * 128:(t + 1) * 128] = high
        t_lo[:, t * 128:(t + 1) * 128] = (turned - high.astype(jnp.float32)).astype(jnp.bfloat16)

    for t in range(8):
        split_target(t)
    top_y[...] = jnp.full(top_y.shape, -1e30, jnp.float32)
    sum_y[...] = jnp.zeros(sum_y.shape, jnp.float32)
    eye = lax.broadcasted_iota(jnp.int32, (128, 128), 0) == lax.broadcasted_iota(jnp.int32, (128, 128), 1)

    def unit_of(j, i):
        near = jnp.where(j < 2, b, mate_b) * 8 + (j % 2) * 4 + i
        whole = jnp.where(j == 4, q_x, q_d) * 2 + i % 2
        split = (q_y if i % 2 == 0 else q_z) * 2 + (j - 5)
        far = (opp_b if i < 2 else opp_mate_b) * 8 + jnp.where((j == 5) | (j == 6), split, whole)
        return jnp.where(j < 4, near, far)

    def events(i, place):
        def when(slot, act):
            if slot % 6 == place and slot >= 0:
                pl.when(i == slot // 6)(act)

        def send_x(k):
            for copy in x_copies(k, b):
                copy.start()

        def relay(k):
            for copy in x_copies(k, opp_b):
                copy.wait_recv()
            for copy in (*y_copies(k, q_x), *z_copies(k, q_x)):
                copy.start()
            if k % 2 == 1:
                mate_copy(0, k // 2, opp_b).start()

        def cross(u):
            for k in (2 * u, 2 * u + 1):
                for copy in (*y_copies(k, q_y), *z_copies(k, q_z)):
                    copy.wait_recv()
            for copy in cross_copies(u, q_z, q_y):
                copy.start()
            mate_copy(1, u, opp_b).start()
            mate_copy(2, u, opp_b).start()

        def crossed(u):
            for copy in cross_copies(u, q_d, q_d):
                copy.wait_recv()
            mate_copy(3, u, opp_b).start()

        def needed(j):
            for part, u in (((0, 0), (0, 1)), ((1, 0), (2, 0)), ((1, 1), (2, 1)), ((3, 0), (3, 1)))[j]:
                mate_copy(part, u, opp_mate_b).wait_recv()

        def mate_needed():
            for part in range(2):
                own_copy(part, mate_b).wait_recv()
            for part, block in enumerate((mate_b, opp_b, opp_mate_b)):
                sharp_copy(part, block, sharp_to[part]).wait_recv()

        for k in range(4):
            when(X_SLOT[k], lambda k=k: send_x(k))
        for k in range(4):
            when(RELAY_SLOT[k], lambda k=k: relay(k))
        for u in range(2):
            when(CROSS_SLOT[u], lambda u=u: cross(u))
            when(MATE_SLOT[u], lambda u=u: crossed(u))
        for j in range(4):
            when(ROUND_SLOT[j], lambda j=j: needed(j))
        when(6, mate_needed)

    def convert(j):
        for i in range(4):
            rows = srcall[pl.ds(pl.multiple_of(unit_of(j, i) * UNIT, UNIT), UNIT), :]
            high = rows.astype(jnp.bfloat16)
            s_hi[i * UNIT:(i + 1) * UNIT, :] = high
            s_lo[i * UNIT:(i + 1) * UNIT, :] = (rows - high.astype(jnp.float32)).astype(jnp.bfloat16)

    def peaks(j, held):
        scale = tsharp_ref[...] * LOG2E
        old = top_y[...]
        new = jnp.maximum(old, scale * jnp.max(held[...], axis=0, keepdims=True))
        sum_y[...] = sum_y[...] * jnp.exp2(old - new)
        top_y[...] = new
        for i in range(4):
            here = slice(i * UNIT, (i + 1) * UNIT)
            row = jnp.broadcast_to(sharp_all[unit_of(j, i)] * LOG2E, (128, 128))
            column = jnp.sum(jnp.where(eye, row, 0.0), axis=1, keepdims=True)
            scale_x[here, :] = column
            peak_x[here, :] = jnp.max(held[here, :] * column, axis=1, keepdims=True)

    def target_sums(j, held):
        scale = tsharp_ref[...] * LOG2E
        sum_y[...] += jnp.sum(jnp.exp2(held[...] * scale - top_y[...]), axis=0, keepdims=True)

    def keep(j, held):
        for i in range(4):
            at_unit = pl.ds(pl.multiple_of(unit_of(j, i) * UNIT, UNIT), UNIT)
            for part in range(8):
                cos[part, at_unit, :] = held[i * UNIT:(i + 1) * UNIT, part * 128:(part + 1) * 128]

    def source_sums(j, held):
        for i in range(4):
            here = slice(i * UNIT, (i + 1) * UNIT)
            peak = peak_x[here, :]
            mass = jnp.sum(jnp.exp2(held[here, :] * scale_x[here, :] - peak), axis=1, keepdims=True)
            total = jnp.broadcast_to(peak + log2(mass), (128, 128))
            lse[unit_of(j, i)] = jnp.sum(jnp.where(eye, total, 0.0), axis=0, keepdims=True)

    def dot(left, right):
        return jnp.dot(left[...], right[...], preferred_element_type=jnp.float32)

    def pair_step(i, _):
        for half, (now, before) in enumerate(((buf_a, buf_b), (buf_b, buf_a))):
            j = 2 * i + half
            last = jnp.maximum(j - 1, 0)
            events(i, 3 * half)
            convert(j)
            now[...] = dot(s_hi, t_hi)
            peaks(last, before)
            events(i, 3 * half + 1)
            now[...] += dot(s_hi, t_lo)
            target_sums(last, before)
            keep(last, before)
            events(i, 3 * half + 2)
            now[...] += dot(s_lo, t_hi)
            source_sums(last, before)
            if half == 0:
                @pl.when(i == 0)
                def _():
                    top_y[...] = jnp.full(top_y.shape, -1e30, jnp.float32)
                    sum_y[...] = jnp.zeros(sum_y.shape, jnp.float32)
        return 0

    buf_b[...] = jnp.zeros(buf_b.shape, jnp.float32)
    pl.semaphore_wait(barrier, 31)
    for copy in x_copies(0, b):
        copy.start()
    sharp_all[pl.ds(b * 8, 8)] = sharp_in[...]
    sharp_to = ((mate_b, w), (opp_b, w), (opp_mate_b, w))
    for i, where in enumerate(sharp_to):
        sharp_copy(i, b, where).start()
    own_copy(0, b).start()
    own_copy(1, b).start()
    lax.fori_loop(0, 4, pair_step, 0)
    peaks(7, buf_b)
    source_sums(7, buf_b)

    def to_a(d):
        owner = (me_a + d) % 16
        return pltpu.make_async_remote_copy(
            src_ref=lse.at[pl.ds(owner * 2, 2)], dst_ref=part_a.at[d - 1], send_sem=a_send, recv_sem=a_recv,
            device_id=peer_a(d), device_id_type=MESH,
        )

    def start_a(d, _):
        to_a(d).start()
        return 0

    lax.fori_loop(1, 16, start_a, 0)
    target_sums(7, buf_b)
    keep(7, buf_b)

    def pick(t):
        def body(i, _):
            for u in range(16):
                slot = i * 16 + u
                picked[pl.ds(slot, 1), :] = cos[t, pl.ds(cand_smem[t, slot], 1), :]
            return 0

        lax.fori_loop(0, 8, body, 0)
        want = lax.broadcasted_iota(jnp.int32, (128, 128), 0) == ctgt_ref[t:t + 1, :]
        pair8[t:t + 1, :] = jnp.sum(jnp.where(want, picked[...].T, 0.0), axis=0, keepdims=True)

    for t in range(4):
        pick(t)
    pltpu.make_async_copy(part_a, part_a, a_recv).wait()
    mine = lse[pl.ds(me_a * 2, 2)]
    part_b[0] = combine(jnp.concatenate([part_a[...], mine[None]], axis=0))

    def start_b(d, _):
        pltpu.make_async_remote_copy(
            src_ref=part_b.at[0], dst_ref=part_b.at[d], send_sem=b_send, recv_sem=b_recv,
            device_id=peer_b(d), device_id_type=MESH,
        ).start()
        return 0

    lax.fori_loop(1, 16, start_b, 0)
    for t in range(4, 8):
        pick(t)
    scale_y = tsharp_ref[...]
    bwd = (top_y[...] + log2(sum_y[...]) - 4.0) * LN2 / scale_y
    for t in range(8):
        bwd8[t:t + 1, :] = bwd[:, t * 128:(t + 1) * 128]
    pltpu.make_async_copy(part_b.at[pl.ds(1, 15)], part_b.at[pl.ds(1, 15)], b_recv).wait()
    fwd_all[me_a] = (combine(part_b[...]) - 4.0) * LN2 / sharp_all[pl.ds(me_a * 2, 2)]

    def start_c(d, _):
        there = fwd_all.at[me_a]
        pltpu.make_async_remote_copy(
            src_ref=there, dst_ref=there, send_sem=c_send, recv_sem=c_recv,
            device_id=peer_a(d), device_id_type=MESH,
        ).start()
        return 0

    lax.fori_loop(1, 16, start_c, 0)

    for k in range(4):
        for copy in (*x_copies(k, b), *y_copies(k, q_x), *z_copies(k, q_x)):
            copy.wait_send()
    for u in range(2):
        for copy in cross_copies(u, q_z, q_y):
            copy.wait_send()
        for i in range(4):
            mate_copy(i, u, opp_b).wait_send()
    for i in range(2):
        own_copy(i, b).wait_send()
    for i, where in enumerate(sharp_to):
        sharp_copy(i, b, where).wait_send()
    pltpu.make_async_copy(part_a, part_a, a_send).wait()
    pltpu.make_async_copy(part_b.at[pl.ds(1, 15)], part_b.at[pl.ds(1, 15)], b_send).wait()

    def lookup(table, index):
        return jnp.take_along_axis(table, index, axis=1, mode="promise_in_bounds")

    bwd_cand = lookup(bwd8[...], ctgt_ref[...])
    sources = cand_ref[...]
    low, high = sources % 128, sources // 128
    counts = jnp.zeros((8, 128), jnp.int32)
    tile_id = lax.broadcasted_iota(jnp.int32, (8, 128), 0)
    for t in range(8):
        counts = jnp.where(tile_id == t, count_ref[t], counts)
    valid = lax.broadcasted_iota(jnp.int32, (8, 128), 1) < counts

    pltpu.make_async_copy(part_a, part_a, c_recv).wait()
    pltpu.make_async_copy(part_a, part_a, c_send).wait()
    fwd_cand = jnp.zeros((8, 128), jnp.float32)
    for r in range(32):
        row = jnp.broadcast_to(fwd_all[r // 2, r % 2], (8, 128))
        fwd_cand = jnp.where(high == r, lookup(row, low), fwd_cand)
    denom = jnp.maximum(0.5 * (fwd_cand + bwd_cand), 0.5)
    out_ref[...] = jnp.where(valid, pair8[...] / denom, 0.0)


def per_device(src_emb, src_sharp, tgt_emb, tgt_sharp, cand_src, cand_tgt, cand_count):
    vmem = pl.BlockSpec(memory_space=pltpu.VMEM)
    smem = pl.BlockSpec(memory_space=pltpu.SMEM)
    hbm = pl.BlockSpec(memory_space=pl.ANY)
    dma = pltpu.SemaphoreType.DMA
    f32, bf16 = jnp.float32, jnp.bfloat16
    return pl.pallas_call(
        kernel,
        out_shape=jax.ShapeDtypeStruct((8, 128), f32),
        in_specs=[hbm, vmem, hbm, vmem, smem, vmem, vmem, smem],
        out_specs=vmem,
        scratch_shapes=[
            pltpu.VMEM((4 * ROWS, D), f32),
            pltpu.VMEM((8, 4 * ROWS, 128), f32),
            pltpu.VMEM((ROWS, D), f32),
            pltpu.VMEM((D, ROWS), bf16),
            pltpu.VMEM((D, ROWS), bf16),
            pltpu.VMEM((HALF, D), bf16),
            pltpu.VMEM((HALF, D), bf16),
            pltpu.VMEM((32, 1, 128), f32),
            pltpu.VMEM((32, 1, 128), f32),
            pltpu.VMEM((15, 2, 1, 128), f32),
            pltpu.VMEM((16, 2, 1, 128), f32),
            pltpu.VMEM((16, 2, 1, 128), f32),
            pltpu.VMEM((HALF, ROWS), f32),
            pltpu.VMEM((HALF, ROWS), f32),
            pltpu.VMEM((HALF, 1), f32),
            pltpu.VMEM((HALF, 1), f32),
            pltpu.VMEM((1, ROWS), f32),
            pltpu.VMEM((1, ROWS), f32),
            pltpu.VMEM((8, 128), f32),
            pltpu.VMEM((128, 128), f32),
            pltpu.VMEM((8, 128), f32),
            dma((3,)), dma((2,)), dma((2,)), *[dma((4, 2))] * 6,
            *[dma((2, 2))] * 4, dma((4, 2)), dma((4, 2)), dma((3,)), dma((3,)),
            dma, dma, dma, dma, dma, dma,
        ],
        compiler_params=pltpu.CompilerParams(
            collective_id=0, has_side_effects=True, vmem_limit_bytes=60 * 1024 * 1024
        ),
        cost_estimate=pl.CostEstimate(flops=6 * 4096 * 1024 * 1024, bytes_accessed=8 << 20, transcendentals=8 << 20),
    )(
        src_emb, src_sharp.reshape(8, 1, 128), tgt_emb, tgt_sharp.reshape(1, ROWS),
        cand_src, cand_src, cand_tgt, cand_count,
    )


def solution(mesh):
    placed = (
        P("blk", None),
        P("blk"),
        P(("blk", "wide"), None),
        P(("blk", "wide")),
        P(("blk", "wide"), None),
        P(("blk", "wide"), None),
        P(("blk", "wide")),
    )
    return jax.shard_map(
        per_device, mesh=mesh, in_specs=placed, out_specs=P(("blk", "wide"), None), check_vma=False
    )
```

time: 104 us -> 67.1 us (0.65)
  Pallas kernels: 102 us -> 65.7 us
    pallas_call x1, Pallas kernels: 102 us -> 65.7 us  [per_device(): pl.pallas_call(kernel, out_shape=jax.ShapeDtypeStruct((8, 128), f32), in_...]
where the time goes in v2:
time: 67.1 us; the launch traced here: 67 us
  Pallas kernels  65.7 us (98%)
  local copies, waits for them, and re-layouts  1.28 us (2%)
    pallas_call x1, Pallas kernels, per_device(): pl.pallas_call(kernel, out_shape=jax.ShapeDtypeStruct((8, 128), f32), in_...  65.7 us

profile of v2, /device:TPU:1, one launch (start us, length us, event | category | flops | bytes accessed | tf_op | source)
XLA Modules:
  0.0 67.0 jit_solution(14386649541224429951)
XLA Ops:
  0.0 65.7 %shard_map.73 = f32[8,128]{1,0:T(8,128)} custom-call(f32[1024,1024]{1,0:T(8,128)} %src_hbm.1, f32[8,1,128]{2,1,0:T(1,128)} %bitcast.2, f32[1024,1024]{1,0:T(8,128)} %tgt_hbm.1, f32[1,1024]{1,0:T(1,128)} %bitcast.3, s32[8,128]{1,0:T(8,128)} %cand_ref.1, s32[8,128]{1,0:T(8,128)} %cand_ref.1, s32[8,128]{1,0:T(8,128)} %ctgt_ref.1, s32[8]{0:T(128)} %count_ref.1), custom_call_target="tpu_custom_call" | custom-call | flops 25769803776 | bytes 8388608 | tf_op jit(solution)/shard_map/pallas_call | solution.py:415
  65.7 1.3 %copy.9 = f32[8,128]{1,0:T(8,128)} copy(f32[8,128]{1,0:T(8,128)} %shard_map.73) | data formatting | bytes 8192

commit v3 on v2

--- a/solution.py
+++ b/solution.py
@@ -14,10 +14,12 @@
 HALF = 512
 QUARTER = 256
 PIECE = 32
-X_SLOT = (-1, 2, 4, 5)
+GROUPS = 1
+GROUP = ROWS // GROUPS
+X_SLOT = (-1, 2, 4, 5, 7, 9)
 RELAY_SLOT = (5, 7, 9, 10)
-CROSS_SLOT = (12, 15)
-MATE_SLOT = (17, 20)
+CROSS_SLOT = 12
+MATE_SLOT = (14, 15, 17)
 ROUND_SLOT = (12, 15, 18, 21)
 
 
@@ -98,13 +100,13 @@
 
     def unit_rows(ref, start):
         def body(i, _):
-            at_rows = pl.ds(pl.multiple_of(start + i * 32, 32), 32)
+            at_rows = pl.ds(pl.multiple_of(start + i * 128, 128), 128)
             rows = ref[at_rows, :]
             norm = jnp.sum(rows * rows, axis=1, keepdims=True) + 1e-06
-            ref[at_rows, :] = rows / jnp.sqrt(norm)
+            ref[at_rows, :] = rows * (1.0 / jnp.sqrt(norm))
             return 0
 
-        lax.fori_loop(0, HALF // 32, body, 0)
+        lax.fori_loop(0, HALF // 128, body, 0)
 
     def remote(rows, count, send, recv, where):
         there = srcall.at[pl.ds(pl.multiple_of(rows, PIECE), count)]
@@ -125,7 +127,11 @@
     along_x, along_y, along_z = (x_next, x_prev), (y_next, y_prev), (z_next, z_prev)
 
     def x_copies(k, block):
-        return both(block, q_x, k, x_send, x_recv, along_x)
+        quarter, at_k = (q_x, k) if k < 4 else (q_d, k - 2)
+        return tuple(
+            remote(piece(block, quarter, at_k, side), PIECE, x_send.at[k, side], x_recv.at[k, side], along_x[side])
+            for side in range(2)
+        )
 
     def y_copies(k, quarter):
         return both(opp_b, quarter, k, y_send, y_recv, along_y)
@@ -133,10 +139,10 @@
     def z_copies(k, quarter):
         return both(opp_b, quarter, k, z_send, z_recv, along_z)
 
-    def cross_copies(u, over_y, over_z):
+    def cross_copies(over_y, over_z):
         return (
-            *(remote(piece(opp_b, over_y, 2 * u, side), PIECE, dy_send.at[u, side], dy_recv.at[u, side], along_y[side]) for side in range(2)),
-            *(remote(piece(opp_b, over_z, 2 * u + 1, side), PIECE, dz_send.at[u, side], dz_recv.at[u, side], along_z[side]) for side in range(2)),
+            *(remote(piece(opp_b, over_y, 0, side), PIECE, dy_send.at[side], dy_recv.at[side], along_y[side]) for side in range(2)),
+            *(remote(piece(opp_b, over_z, 1, side), PIECE, dz_send.at[side], dz_recv.at[side], along_z[side]) for side in range(2)),
         )
 
     quarters = (q_x, q_y, q_z, q_d)
@@ -163,7 +169,7 @@
     def split_target(t):
         rows = tgt_raw[t * 128:(t + 1) * 128, :]
         norm = jnp.sum(rows * rows, axis=1, keepdims=True) + 1e-06
-        turned = (rows / jnp.sqrt(norm)).T
+        turned = (rows * (1.0 / jnp.sqrt(norm))).T
         high = turned.astype(jnp.bfloat16)
         t_hi[:, t * 128:(t + 1) * 128] = high
         t_lo[:, t * 128:(t + 1) * 128] = (turned - high.astype(jnp.float32)).astype(jnp.bfloat16)
@@ -198,19 +204,35 @@
             if k % 2 == 1:
                 mate_copy(0, k // 2, opp_b).start()
 
-        def cross(u):
+        def arrived(u):
             for k in (2 * u, 2 * u + 1):
                 for copy in (*y_copies(k, q_y), *z_copies(k, q_z)):
                     copy.wait_recv()
-            for copy in cross_copies(u, q_z, q_y):
-                copy.start()
+
+        def to_mate(u):
             mate_copy(1, u, opp_b).start()
             mate_copy(2, u, opp_b).start()
 
-        def crossed(u):
-            for copy in cross_copies(u, q_d, q_d):
+        def cross():
+            arrived(0)
+            for copy in cross_copies(q_z, q_y):
+                copy.start()
+            to_mate(0)
+
+        def direct():
+            for k in (4, 5):
+                for copy in x_copies(k, opp_b):
+                    copy.wait_recv()
+            mate_copy(3, 1, opp_b).start()
+
+        def last_relayed():
+            arrived(1)
+            to_mate(1)
+
+        def crossed():
+            for copy in cross_copies(q_d, q_d):
                 copy.wait_recv()
-            mate_copy(3, u, opp_b).start()
+            mate_copy(3, 0, opp_b).start()
 
         def needed(j):
             for part, u in (((0, 0), (0, 1)), ((1, 0), (2, 0)), ((1, 1), (2, 1)), ((3, 0), (3, 1)))[j]:
@@ -222,13 +244,13 @@
             for part, block in enumerate((mate_b, opp_b, opp_mate_b)):
                 sharp_copy(part, block, sharp_to[part]).wait_recv()
 
-        for k in range(4):
+        for k in range(6):
             when(X_SLOT[k], lambda k=k: send_x(k))
         for k in range(4):
             when(RELAY_SLOT[k], lambda k=k: relay(k))
-        for u in range(2):
-            when(CROSS_SLOT[u], lambda u=u: cross(u))
-            when(MATE_SLOT[u], lambda u=u: crossed(u))
+        when(CROSS_SLOT, cross)
+        for slot, act in zip(MATE_SLOT, (direct, last_relayed, crossed)):
+            when(slot, act)
         for j in range(4):
             when(ROUND_SLOT[j], lambda j=j: needed(j))
         when(6, mate_needed)
@@ -240,39 +262,38 @@
             s_hi[i * UNIT:(i + 1) * UNIT, :] = high
             s_lo[i * UNIT:(i + 1) * UNIT, :] = (rows - high.astype(jnp.float32)).astype(jnp.bfloat16)
 
-    def peaks(j, held):
-        scale = tsharp_ref[...] * LOG2E
-        old = top_y[...]
-        new = jnp.maximum(old, scale * jnp.max(held[...], axis=0, keepdims=True))
-        sum_y[...] = sum_y[...] * jnp.exp2(old - new)
-        top_y[...] = new
-        for i in range(4):
-            here = slice(i * UNIT, (i + 1) * UNIT)
-            row = jnp.broadcast_to(sharp_all[unit_of(j, i)] * LOG2E, (128, 128))
-            column = jnp.sum(jnp.where(eye, row, 0.0), axis=1, keepdims=True)
-            scale_x[here, :] = column
-            peak_x[here, :] = jnp.max(held[here, :] * column, axis=1, keepdims=True)
-
-    def target_sums(j, held):
-        scale = tsharp_ref[...] * LOG2E
-        sum_y[...] += jnp.sum(jnp.exp2(held[...] * scale - top_y[...]), axis=0, keepdims=True)
-
-    def keep(j, held):
-        for i in range(4):
-            at_unit = pl.ds(pl.multiple_of(unit_of(j, i) * UNIT, UNIT), UNIT)
-            for part in range(8):
-                cos[part, at_unit, :] = held[i * UNIT:(i + 1) * UNIT, part * 128:(part + 1) * 128]
-
-    def source_sums(j, held):
-        for i in range(4):
-            here = slice(i * UNIT, (i + 1) * UNIT)
-            peak = peak_x[here, :]
-            mass = jnp.sum(jnp.exp2(held[here, :] * scale_x[here, :] - peak), axis=1, keepdims=True)
-            total = jnp.broadcast_to(peak + log2(mass), (128, 128))
-            lse[unit_of(j, i)] = jnp.sum(jnp.where(eye, total, 0.0), axis=0, keepdims=True)
-
-    def dot(left, right):
-        return jnp.dot(left[...], right[...], preferred_element_type=jnp.float32)
+    def target_peaks(held, cols):
+        scale = tsharp_ref[:, cols] * LOG2E
+        old = top_y[:, cols]
+        new = jnp.maximum(old, scale * jnp.max(held[:, cols], axis=0, keepdims=True))
+        sum_y[:, cols] = sum_y[:, cols] * jnp.exp2(old - new)
+        top_y[:, cols] = new
+
+    def source_peaks(j, held, i):
+        here = slice(i * UNIT, (i + 1) * UNIT)
+        row = jnp.broadcast_to(sharp_all[unit_of(j, i)] * LOG2E, (128, 128))
+        column = jnp.sum(jnp.where(eye, row, 0.0), axis=1, keepdims=True)
+        scale_x[here, :] = column
+        peak_x[here, :] = jnp.max(held[here, :] * column, axis=1, keepdims=True)
+
+    def target_sums(held, cols):
+        scale = tsharp_ref[:, cols] * LOG2E
+        sum_y[:, cols] += jnp.sum(jnp.exp2(held[:, cols] * scale - top_y[:, cols]), axis=0, keepdims=True)
+
+    def keep(j, held, i):
+        at_unit = pl.ds(pl.multiple_of(unit_of(j, i) * UNIT, UNIT), UNIT)
+        for part in range(8):
+            cos[part, at_unit, :] = held[i * UNIT:(i + 1) * UNIT, part * 128:(part + 1) * 128]
+
+    def source_sums(j, held, i):
+        here = slice(i * UNIT, (i + 1) * UNIT)
+        peak = peak_x[here, :]
+        mass = jnp.sum(jnp.exp2(held[here, :] * scale_x[here, :] - peak), axis=1, keepdims=True)
+        total = jnp.broadcast_to(peak + log2(mass), (128, 128))
+        lse[unit_of(j, i)] = jnp.sum(jnp.where(eye, total, 0.0), axis=0, keepdims=True)
+
+    def dot(left, right, cols):
+        return jnp.dot(left[...], right[:, cols], preferred_element_type=jnp.float32)
 
     def pair_step(i, _):
         for half, (now, before) in enumerate(((buf_a, buf_b), (buf_b, buf_a))):
@@ -280,15 +301,25 @@
             last = jnp.maximum(j - 1, 0)
             events(i, 3 * half)
             convert(j)
-            now[...] = dot(s_hi, t_hi)
-            peaks(last, before)
+            for g in range(GROUPS):
+                cols = slice(g * GROUP, (g + 1) * GROUP)
+                now[:, cols] = dot(s_hi, t_hi, cols)
+                target_peaks(before, cols)
+                for part in range(g * 4 // GROUPS, (g + 1) * 4 // GROUPS):
+                    source_peaks(last, before, part)
             events(i, 3 * half + 1)
-            now[...] += dot(s_hi, t_lo)
-            target_sums(last, before)
-            keep(last, before)
+            for g in range(GROUPS):
+                cols = slice(g * GROUP, (g + 1) * GROUP)
+                now[:, cols] += dot(s_hi, t_lo, cols)
+                target_sums(before, cols)
+                for part in range(g * 4 // GROUPS, (g + 1) * 4 // GROUPS):
+                    keep(last, before, part)
             events(i, 3 * half + 2)
-            now[...] += dot(s_lo, t_hi)
-            source_sums(last, before)
+            for g in range(GROUPS):
+                cols = slice(g * GROUP, (g + 1) * GROUP)
+                now[:, cols] += dot(s_lo, t_hi, cols)
+                for part in range(g * 4 // GROUPS, (g + 1) * 4 // GROUPS):
+                    source_sums(last, before, part)
             if half == 0:
                 @pl.when(i == 0)
                 def _():
@@ -307,8 +338,9 @@
     own_copy(0, b).start()
     own_copy(1, b).start()
     lax.fori_loop(0, 4, pair_step, 0)
-    peaks(7, buf_b)
-    source_sums(7, buf_b)
+    for part in range(4):
+        source_peaks(7, buf_b, part)
+        source_sums(7, buf_b, part)
 
     def to_a(d):
         owner = (me_a + d) % 16
@@ -322,8 +354,10 @@
         return 0
 
     lax.fori_loop(1, 16, start_a, 0)
-    target_sums(7, buf_b)
-    keep(7, buf_b)
+    target_peaks(buf_b, slice(0, ROWS))
+    target_sums(buf_b, slice(0, ROWS))
+    for part in range(4):
+        keep(7, buf_b, part)
 
     def pick(t):
         def body(i, _):
@@ -369,13 +403,16 @@
 
     lax.fori_loop(1, 16, start_c, 0)
 
+    for k in range(6):
+        for copy in x_copies(k, b):
+            copy.wait_send()
     for k in range(4):
-        for copy in (*x_copies(k, b), *y_copies(k, q_x), *z_copies(k, q_x)):
+        for copy in (*y_copies(k, q_x), *z_copies(k, q_x)):
             copy.wait_send()
-    for u in range(2):
-        for copy in cross_copies(u, q_z, q_y):
-            copy.wait_send()
-        for i in range(4):
+    for copy in cross_copies(q_z, q_y):
+        copy.wait_send()
+    for i in range(4):
+        for u in range(2):
             mate_copy(i, u, opp_b).wait_send()
     for i in range(2):
         own_copy(i, b).wait_send()
@@ -439,8 +476,8 @@
             pltpu.VMEM((8, 128), f32),
             pltpu.VMEM((128, 128), f32),
             pltpu.VMEM((8, 128), f32),
-            dma((3,)), dma((2,)), dma((2,)), *[dma((4, 2))] * 6,
-            *[dma((2, 2))] * 4, dma((4, 2)), dma((4, 2)), dma((3,)), dma((3,)),
+            dma((3,)), dma((2,)), dma((2,)), dma((6, 2)), dma((6, 2)), *[dma((4, 2))] * 4,
+            *[dma((2,))] * 4, dma((4, 2)), dma((4, 2)), dma((3,)), dma((3,)),
             dma, dma, dma, dma, dma, dma,
         ],
         compiler_params=pltpu.CompilerParams(

time: 67.1 us -> 65.4 us (0.975)
  Pallas kernels: 65.7 us -> 64 us
    pallas_call x1, Pallas kernels: 65.7 us -> 64 us  [per_device(): pl.pallas_call(kernel, out_shape=jax.ShapeDtypeStruct((8, 128), f32), in_...]
where the time goes in v3:
time: 65.4 us; the launch traced here: 65.2 us
  Pallas kernels  64 us (98%)
  local copies, waits for them, and re-layouts  1.28 us (2%)
    pallas_call x1, Pallas kernels, per_device(): pl.pallas_call(kernel, out_shape=jax.ShapeDtypeStruct((8, 128), f32), in_...  64 us

profile of v3, /device:TPU:1, one launch (start us, length us, event | category | flops | bytes accessed | tf_op | source)
XLA Modules:
  0.0 65.2 jit_solution(11187117841441802297)
XLA Ops:
  0.0 64.0 %shard_map.73 = f32[8,128]{1,0:T(8,128)} custom-call(f32[1024,1024]{1,0:T(8,128)} %src_hbm.1, f32[8,1,128]{2,1,0:T(1,128)} %bitcast.2, f32[1024,1024]{1,0:T(8,128)} %tgt_hbm.1, f32[1,1024]{1,0:T(1,128)} %bitcast.3, s32[8,128]{1,0:T(8,128)} %cand_ref.1, s32[8,128]{1,0:T(8,128)} %cand_ref.1, s32[8,128]{1,0:T(8,128)} %ctgt_ref.1, s32[8]{0:T(128)} %count_ref.1), custom_call_target="tpu_custom_call" | custom-call | flops 25769803776 | bytes 8388608 | tf_op jit(solution)/shard_map/pallas_call | solution.py:452
  64.0 1.3 %copy.9 = f32[8,128]{1,0:T(8,128)} copy(f32[8,128]{1,0:T(8,128)} %shard_map.73) | data formatting | bytes 8192
